TPU v7x, 512 devices: a whole 4x8x8 slice. The times are simulated.
512 devices in a mesh: rows: 64 (over x, z, core), grp: 8 (over y).
Axes of the slice: x: 4, y: 8, z: 8, core: 2. Of those that a mesh axis runs over, the one named last changes fastest.
Arguments:
- matrix: float32 [131072, 768], P(('rows', 'grp')), as said below
- sketch: float32 [768, 256], replicated, may hold values from -6 to 6
Outputs:
- basis_scaled: float32 [131072, 256], P(('rows', 'grp'))
- coeffs: float32 [256, 768], P(None, 'rows')
Inputs may be any that keep to these rules, and one draw needn't show every extreme that they name: Rows of the matrix have independent scales; entries are bounded by 48 / sqrt(131072) in magnitude.
All inputs are finite; a program needn't handle non-finite values.
Results may differ from a plain program's by a relative error of at most 0.0003.
Values sent between devices are 32-bit elements; how exact they have to be, the bound alone decides.
A program may use at most 64 MiB of HBM per device.

v0:
```python
import jax
import jax.numpy as jnp
from jax import lax
from jax.sharding import PartitionSpec as P


def mult(left, right):
    return jnp.dot(left, right, precision=lax.Precision.HIGHEST, preferred_element_type=jnp.float32)


def column_slice(whole):
    width = whole.shape[1] // lax.axis_size("rows")
    return lax.dynamic_slice_in_dim(whole, lax.axis_index("rows") * width, width, 1)


def reduce_columns(partial_sum):
    whole = lax.psum(partial_sum, ("rows", "grp"))
    return column_slice(whole)


def shards(matrix, sketch):
    total_rows = matrix.shape[0] * lax.axis_size("rows") * lax.axis_size("grp")
    proj = mult(matrix, sketch)
    power = lax.psum(mult(matrix.T, proj), ("rows", "grp"))
    range_rows = mult(matrix, power)
    local_gram = mult(range_rows.T, range_rows)
    gram = lax.psum(local_gram, ("rows", "grp"))
    lower = jnp.linalg.cholesky(gram)
    basis = jax.scipy.linalg.solve_triangular(lower, range_rows.T, lower=True).T
    coeffs = reduce_columns(mult(basis.T, matrix))
    scaled = basis * jnp.sqrt(jnp.float32(total_rows))
    return (scaled, coeffs)


def solution(mesh):
    placed = (P(("rows", "grp"), None), P())
    return jax.shard_map(
        shards,
        mesh=mesh,
        in_specs=placed,
        out_specs=(P(("rows", "grp"), None), P(None, "rows")),
        check_vma=False,
    )
```

profile of v0, /device:TPU:1, one launch (start us, length us, event | category | flops | bytes accessed | tf_op | source)
XLA Modules:
  0.0 899.2 jit_solution(7558093129074811227)
XLA Ops:
  7.2 0.0 copy-start
  7.2 0.0 all-reduce.5.cloned.1.call-start
  7.2 1.1 copy-done
  8.3 1.9 fusion.11
  10.2 1.7 convolution_bitcast_fusion
  12.0 0.0 all-reduce.5.cloned.1.call-update
  12.0 0.0 all-reduce.7.cloned.1.call-start
  12.1 277.9 %all-reduce.5.cloned.1.call-done = f32[768,256]{0,1:T(8,128)} async-done(((f32[768,256]{0,1:T(8,128)}), f32[768,256]{0,1:T(8,128)}) %all-reduce.5.cloned.1.call-update) | async-done | bytes 786448 | tf_op jit(solution)/shard_map/psum | solution.py:24
  290.0 2.0 fusion.12
  292.0 1.1 fusion.13
  293.1 0.0 all-reduce.7.cloned.1.call-update
  293.1 0.2 all-reduce.9.cloned.1.call-start
  293.4 265.8 %all-reduce.7.cloned.1.call-done = f32[256,256]{0,1:T(8,128)} async-done(((f32[256,256]{0,1:T(8,128)}), f32[256,256]{0,1:T(8,128)}) %all-reduce.7.cloned.1.call-update) | async-done | bytes 262160 | tf_op jit(solution)/shard_map/psum | solution.py:27
  559.2 0.0 copy-start.1
  559.2 1.1 copy.5
  560.3 0.0 copy-done.1
  560.4 11.7 %cholesky.50 = f32[128,128]{1,0:T(8,128)S(1)} custom-call(f32[128,128]{1,0:T(8,128)S(1)} %cholesky.118), custom_call_target="Cholesky" | custom-call | tf_op jit(solution)/shard_map/jit(cholesky)/cholesky | solution.py:28
  572.2 9.8 %custom-call.15 = f32[1,128,128]{1,2,0:T(8,128)S(1)} custom-call(f32[1,128,128]{2,1,0:T(8,128)S(1)} %get-tuple-element.25), custom_call_target="InvertDiagBlocksLowerTriangular" | custom-call | tf_op jit(solution)/shard_map/jit(cholesky)/cholesky | solution.py:28
  582.0 0.2 constant_dynamic-update-slice_fusion
  582.2 0.3 convolution_subtract_fusion.1
  582.5 11.7 %cholesky.105 = f32[128,128]{1,0:T(8,128)S(1)} custom-call(f32[128,128]{1,0:T(8,128)S(1)} %convolution_subtract_fusion.1), custom_call_target="Cholesky" | custom-call | tf_op jit(solution)/shard_map/jit(cholesky)/cholesky | solution.py:28
  594.2 0.7 compare_reduce_fusion
  596.3 0.1 triangular_solve.57
  596.4 4.3 while.1
  596.6 0.6 fusion.28
  597.2 1.4 bitcast_dynamic-update-slice_fusion.2
  598.7 0.6 fusion.28
  599.3 1.4 bitcast_dynamic-update-slice_fusion.2
  600.7 19.7 %custom-call.16 = f32[2,128,128]{1,2,0:T(8,128)S(1)} custom-call(f32[2,128,128]{2,1,0:T(8,128)S(1)} %get-tuple-element.9), custom_call_target="InvertDiagBlocksLowerTriangular" | custom-call | tf_op jit(solution)/shard_map/jit(_solve_triangular)/triangular_solve | solution.py:29
  620.4 0.3 fusion.2
  620.7 0.3 convolution_subtract_fusion
  621.0 0.3 fusion.5
  621.3 2.3 fusion.1
  623.6 0.0 all-reduce.9.cloned.1.call-update
  623.7 0.8 copy.6
  624.5 266.9 %all-reduce.9.cloned.1.call-done = f32[256,768]{0,1:T(8,128)} async-done(((f32[256,768]{0,1:T(8,128)}), f32[256,768]{0,1:T(8,128)}) %all-reduce.9.cloned.1.call-update) | async-done | bytes 786448 | tf_op jit(solution)/shard_map/psum | solution.py:17
  891.4 1.3 constant_dynamic-slice_fusion.1
  (11 shorter events, 0.2 us)
Async XLA Ops:
  7.2 1.1 copy-start
  7.2 282.8 %all-reduce.5.cloned.1.call-start = ((), (), s32[]{:S(2)}) async-start(), calls=%async_computation | async-start | bytes 1572864 | tf_op jit(solution)/shard_map/psum | solution.py:24
  12.0 547.2 %all-reduce.7.cloned.1.call-start = ((), (), s32[]{:S(2)}) async-start(), calls=%async_computation.1 | async-start | bytes 524288 | tf_op jit(solution)/shard_map/psum | solution.py:27
  293.1 598.3 %all-reduce.9.cloned.1.call-start = ((), (), s32[]{:S(2)}) async-start(), calls=%async_computation.2 | async-start | bytes 1572864 | tf_op jit(solution)/shard_map/psum | solution.py:17
  559.2 1.2 copy-start.1
Sparse Core Ops, SparseCore 0:
  13.0 276.9 all-reduce.4
  295.6 263.5 all-reduce.6
  623.7 267.5 all-reduce.8
where the time goes:
time: 900 us; the launch traced here: 899 us
  waiting for transfers between devices  811 us (90%)
  other arithmetic  53.8 us (6%)
  between operations  15.2 us (2%)
  matrix products  10.4 us (1%)
    psum x1, waiting for transfers between devices, shards(): power = lax.psum(mult(matrix.T, proj), ('rows', 'grp'))  278 us
    psum x1, waiting for transfers between devices, reduce_columns(): whole = lax.psum(partial_sum, ('rows', 'grp'))  267 us
    psum x1, waiting for transfers between devices, shards(): gram = lax.psum(local_gram, ('rows', 'grp'))  266 us
    another operation x6, other arithmetic, shards(): lower = jnp.linalg.cholesky(gram)  34 us
    another operation x3, other arithmetic, shards(): basis = jax.scipy.linalg.solve_triangular(lower, range_rows.T, lower=True).T  19.7 us
  transfers between devices with their start and end apart: 3, of which 3 were waited for; matrix products, arithmetic and copies ran while one was open for 0% of the time, Pallas kernels for 0%

commit v1 on v0

v1 whole, which is shorter than its diff:
```python
import functools
import jax
import jax.numpy as jnp
from jax import lax
from jax.experimental import pallas as pl
from jax.experimental.pallas import tpu as pltpu
from jax.sharding import PartitionSpec as P

MESH = pl.DeviceIdType.MESH
F32 = jnp.float32
BF16 = jnp.bfloat16
NX, NY, NZ = 4, 8, 8
BLOCKS = [(i, j) for i in range(6) for j in range(i, 6)]
LIVE = 336
HELD = 384
PIECE = 24


def split(v):
    high = v.astype(BF16)
    return high, (v - high.astype(F32)).astype(BF16)


NN = (((1,), (0,)), ((), ()))
NT = (((1,), (1,)), ((), ()))
TN = (((0,), (0,)), ((), ()))


def dot3(left, right, dims):
    def one(a, b):
        return lax.dot_general(a, b, dims, preferred_element_type=F32)
    return one(left[0], right[1]) + one(left[1], right[0]) + one(left[0], right[0])


def place(tile):
    share, row = divmod(tile, LIVE // 8)
    return share // NX, share % NX, row * 8


def store_block(part, index, value):
    for t in range(16):
        core, x, row = place(index * 16 + t)
        part[core, x, row:row + 8, :] = value[8 * t:8 * t + 8, :]


def reduce_kernel(a_hbm, g_ref, a_own, part, sib_in, x_in, acc, z_in, y_in, zy, yz, gath,
                  load_sem, sib_s, sib_r, x_s, x_r, z_s, z_r, y_s, y_r, zy_s, zy_r, yz_s, yz_r,
                  zg_s, zg_r, yg_s, yg_r, xg_s, xg_r, fw_s, fw_r):
    r = lax.axis_index("rows")
    y = lax.axis_index("grp")
    x, z, c = r // 16, lax.rem(r // 2, 8), lax.rem(r, 2)

    def dev(xx, yy, zz, cc):
        return ((xx * NZ + zz) * 2 + cc, yy)

    def other(axis, k):
        if axis == "x":
            return lax.rem(x + k, NX), dev(lax.rem(x + k, NX), y, z, c)
        if axis == "y":
            return lax.rem(y + k, NY), dev(x, lax.rem(y + k, NY), z, c)
        return lax.rem(z + k, NZ), dev(x, y, lax.rem(z + k, NZ), c)

    sibling = dev(x, y, z, 1 - c)
    barrier = pltpu.get_barrier_semaphore()
    pl.semaphore_signal(barrier, inc=1, device_id=sibling, device_id_type=MESH)
    for axis, n in (("x", NX), ("y", NY), ("z", NZ)):
        for k in range(1, n):
            pl.semaphore_signal(barrier, inc=1, device_id=other(axis, k)[1], device_id_type=MESH)
    load = pltpu.make_async_copy(a_hbm, a_own, load_sem)
    load.start()
    load.wait()

    def copy(src, dst, s, rr, to):
        return pltpu.make_async_remote_copy(src_ref=src, dst_ref=dst, send_sem=s, recv_sem=rr,
                                            device_id=to, device_id_type=MESH)

    halves = [split(a_own[:, 128 * i:128 * i + 128]) for i in range(6)]
    for index, (i, j) in enumerate(BLOCKS):
        store_block(part, index, dot3(halves[i], halves[j], TN))

    pl.semaphore_wait(barrier, 1 + (NX - 1) + (NY - 1) + (NZ - 1))
    sent = []
    live = pl.ds(0, LIVE)

    swaps = []
    for k in (1, 2, 3, 0):
        xx = lax.rem(x + k, NX)
        d = copy(part.at[1 - c, xx, live], sib_in.at[xx], sib_s.at[xx], sib_r.at[xx], sibling)
        d.start()
        swaps.append((xx, d))
        sent.append(d)
    for (xx, d), k in zip(swaps[:3], (1, 2, 3)):
        d.wait_recv()
        part[c, xx, 0:LIVE, :] = part[c, xx, 0:LIVE, :] + sib_in[xx]
        out = copy(part.at[c, xx, live], x_in.at[k - 1], x_s.at[k - 1], x_r.at[k - 1], other("x", k)[1])
        out.start()
        sent.append(out)
    swaps[3][1].wait_recv()
    for k in (1, 2, 3):
        copy(part.at[c, x, live], x_in.at[k - 1], x_s.at[k - 1], x_r.at[k - 1], sibling).wait_recv()
    acc[0:LIVE, :] = (part[c, x, 0:LIVE, :] + sib_in[x]) + (x_in[0] + x_in[1] + x_in[2])
    acc[LIVE:HELD, :] = jnp.zeros((HELD - LIVE, 128), F32)

    def piece(half, owner):
        return pl.ds(pl.multiple_of(half * (HELD // 2) + owner * PIECE, 8), PIECE)

    for k in range(1, 8):
        zz, to = other("z", k)
        d = copy(acc.at[piece(0, zz)], z_in.at[k - 1], z_s.at[k - 1], z_r.at[k - 1], to)
        d.start()
        yy, to = other("y", k)
        e = copy(acc.at[piece(1, yy)], y_in.at[k - 1], y_s.at[k - 1], y_r.at[k - 1], to)
        e.start()
        sent += [d, e]
    zsum = acc[piece(0, z), :]
    ysum = acc[piece(1, y), :]
    for k in range(1, 8):
        copy(acc.at[piece(0, z)], z_in.at[k - 1], z_s.at[k - 1], z_r.at[k - 1], sibling).wait_recv()
        zsum += z_in[k - 1]
    zy[y] = zsum
    for k in range(1, 8):
        _, to = other("y", k)
        d = copy(zy.at[y], zy.at[y], zy_s.at[k - 1], zy_r.at[y], to)
        d.start()
        sent.append(d)
    for k in range(1, 8):
        copy(acc.at[piece(1, y)], y_in.at[k - 1], y_s.at[k - 1], y_r.at[k - 1], sibling).wait_recv()
        ysum += y_in[k - 1]
    yz[z] = ysum
    for k in range(1, 8):
        _, to = other("z", k)
        d = copy(yz.at[z], yz.at[z], yz_s.at[k - 1], yz_r.at[z], to)
        d.start()
        sent.append(d)
    for k in range(1, 8):
        yy, _ = other("y", k)
        copy(zy.at[yy], zy.at[yy], zy_s.at[k - 1], zy_r.at[yy], sibling).wait_recv()
    mine = gath.at[c, x]
    total = zy[0]
    for k in range(1, 8):
        total += zy[k]
    gath[c, x, piece(0, z), :] = total
    for k in range(1, 8):
        _, to = other("z", k)
        d = copy(mine.at[piece(0, z)], mine.at[piece(0, z)], zg_s.at[k - 1], zg_r.at[z], to)
        d.start()
        sent.append(d)
    for k in range(1, 8):
        zz, _ = other("z", k)
        copy(yz.at[zz], yz.at[zz], yz_s.at[k - 1], yz_r.at[zz], sibling).wait_recv()
    total = yz[0]
    for k in range(1, 8):
        total += yz[k]
    gath[c, x, piece(1, y), :] = total
    for k in range(1, 8):
        _, to = other("y", k)
        d = copy(mine.at[piece(1, y)], mine.at[piece(1, y)], yg_s.at[k - 1], yg_r.at[y], to)
        d.start()
        sent.append(d)
    for k in range(1, 8):
        zz, _ = other("z", k)
        copy(mine.at[piece(0, zz)], mine.at[piece(0, zz)], zg_s.at[k - 1], zg_r.at[zz], sibling).wait_recv()
    for k in range(1, 8):
        yy, _ = other("y", k)
        copy(mine.at[piece(1, yy)], mine.at[piece(1, yy)], yg_s.at[k - 1], yg_r.at[yy], sibling).wait_recv()

    quarter = gath.at[c, x, live]
    for k in (1, 2, 3):
        d = copy(quarter, quarter, xg_s.at[k - 1], xg_r.at[x], other("x", k)[1])
        d.start()
        sent.append(d)
    d = copy(quarter, quarter, fw_s.at[x], fw_r.at[x], sibling)
    d.start()
    sent.append(d)
    for k in (1, 3, 2):
        xx, _ = other("x", k)
        came = gath.at[c, xx, live]
        copy(came, came, xg_s.at[k - 1], xg_r.at[xx], sibling).wait_recv()
        d = copy(came, came, fw_s.at[xx], fw_r.at[xx], sibling)
        d.start()
        sent.append(d)
    for xx in range(NX):
        came = gath.at[1 - c, xx, live]
        copy(came, came, fw_s.at[xx], fw_r.at[xx], sibling).wait_recv()
    g_ref[...] = gath[:, :, 0:LIVE, :]
    for d in sent:
        d.wait_send()


def dma(*shape):
    return pltpu.SemaphoreType.DMA(shape)


def reduced_gram(matrix):
    rows, cols = matrix.shape
    return pl.pallas_call(
        reduce_kernel,
        out_shape=jax.ShapeDtypeStruct((2, NX, LIVE, 128), F32),
        in_specs=[pl.BlockSpec(memory_space=pl.ANY)],
        out_specs=pl.BlockSpec(memory_space=pltpu.VMEM),
        scratch_shapes=[
            pltpu.VMEM((rows, cols), F32),
            pltpu.VMEM((2, NX, HELD, 128), F32),
            pltpu.VMEM((NX, LIVE, 128), F32),
            pltpu.VMEM((NX - 1, LIVE, 128), F32),
            pltpu.VMEM((HELD, 128), F32),
            pltpu.VMEM((7, PIECE, 128), F32),
            pltpu.VMEM((7, PIECE, 128), F32),
            pltpu.VMEM((8, PIECE, 128), F32),
            pltpu.VMEM((8, PIECE, 128), F32),
            pltpu.VMEM((2, NX, HELD, 128), F32),
            pltpu.SemaphoreType.DMA,
            dma(4), dma(4), dma(3), dma(3), dma(7), dma(7), dma(7), dma(7),
            dma(7), dma(8), dma(7), dma(8), dma(7), dma(8), dma(7), dma(8),
            dma(3), dma(4), dma(4), dma(4),
        ],
        compiler_params=pltpu.CompilerParams(collective_id=0, has_side_effects=True,
                                             vmem_limit_bytes=40 * 1024 * 1024),
        name="reduce_gram",
    )(matrix)


def panel_inverse_8(d, nb):
    n8 = nb // 8
    eye = (lax.broadcasted_iota(jnp.int32, (nb, nb), 0) == lax.broadcasted_iota(jnp.int32, (nb, nb), 1)).astype(F32)
    w = jnp.concatenate([d, eye], 1)
    groups = [w[8 * g:8 * g + 8, :] for g in range(n8)]
    sub = lax.broadcasted_iota(jnp.int32, (8, 128), 0)
    out = [None] * n8
    for g in range(n8):
        cols = {h: [jnp.broadcast_to(groups[h][:, 8 * g + k:8 * g + k + 1], (8, 128)) for k in range(8)] for h in range(g, n8)}
        pivots = []
        for k in range(8):
            row = jnp.broadcast_to(groups[g][k:k + 1, :], (8, 128))
            rows = {m: jnp.broadcast_to(cols[g][m][k:k + 1, :], (8, 128)) for m in range(k, 8)}
            inv = 1.0 / rows[k]
            pivots.append(rows[k])
            q = row * inv
            qs = {m: rows[m] * inv for m in range(k + 1, 8)}
            for h in range(g, n8):
                c = cols[h][k]
                if h == g:
                    c = jnp.where(sub > k, c, 0.0)
                groups[h] = groups[h] - c * q
                for m in range(k + 1, 8):
                    cols[h][m] = cols[h][m] - c * qs[m]
        dia = pivots[7]
        for k in range(7):
            dia = jnp.where(sub == k, pivots[k], dia)
        out[g] = groups[g][:, nb:] * lax.rsqrt(dia)[:, nb:]
    return jnp.concatenate(out, 0)


def cholesky_inverse(gram, linv, nb, panel):
    n = gram.shape[0]
    linv[...] = jnp.zeros((n, n), F32)
    for b in range(n // nb):
        lo, hi = b * nb, (b + 1) * nb
        x = panel(gram[lo:hi, lo:hi], nb)
        xs = split(x)
        if b:
            done = dot3(xs, split(linv[lo:hi, 0:lo]), NN)
            linv[lo:hi, 0:lo] = done
        linv[lo:hi, lo:hi] = x
        if hi < n:
            u = split(dot3(xs, split(gram[lo:hi, hi:n]), NN))
            gram[hi:n, hi:n] = gram[hi:n, hi:n] - dot3(u, u, TN)
            linv[hi:n, 0:hi] = linv[hi:n, 0:hi] - dot3(u, split(linv[lo:hi, 0:hi]), TN)


def load_block(packed, index):
    pieces = []
    for t in range(16):
        core, x, row = place(index * 16 + t)
        pieces.append(packed[core, x, row:row + 8, :])
    return jnp.concatenate(pieces, 0)


def times_gram(left, high, low, dims_of=None):
    strips = []
    for s in range(3):
        lo, hi = 256 * s, 256 * s + 256
        strip = dot3((left[0][:, :hi], left[1][:, :hi]), (high[0:hi, lo:hi], low[0:hi, lo:hi]), NN)
        if hi < 768:
            strip += dot3((left[0][:, hi:], left[1][:, hi:]), (high[lo:hi, hi:], low[lo:hi, hi:]), NT)
        strips.append(strip)
    return jnp.concatenate(strips, 1)


def finish_kernel(scale, packed, a_ref, s_ref, basis_ref, coeffs_ref, high, low, gram, linv):
    r = lax.axis_index("rows")
    for index, (i, j) in enumerate(BLOCKS):
        block = load_block(packed, index)
        h, l = split(block)
        high[128 * i:128 * i + 128, 128 * j:128 * j + 128] = h
        low[128 * i:128 * i + 128, 128 * j:128 * j + 128] = l
        if i // 2 == j // 2 and i != j:
            h, l = split(block.T)
            high[128 * j:128 * j + 128, 128 * i:128 * i + 128] = h
            low[128 * j:128 * j + 128, 128 * i:128 * i + 128] = l
    power = split(times_gram(split(s_ref[...].T), high, low))
    ranged = times_gram(power, high, low)
    halves = split(ranged)
    gram[...] = dot3(halves, power, NT)
    cholesky_inverse(gram, linv, 64, panel_inverse_8)
    inverse = split(linv[...])
    factor = split(dot3(inverse, power, NN))
    basis_ref[...] = dot3(split(a_ref[...]), factor, NT) * scale
    width = coeffs_ref.shape[1]
    row = lax.broadcasted_iota(jnp.int32, (768, 128), 0)
    col = lax.broadcasted_iota(jnp.int32, (768, 128), 1)
    pick = jnp.where(row == col + r * width, 1.0, 0.0).astype(BF16)
    rest = (ranged - halves[0].astype(F32)) - halves[1].astype(F32)
    mine = sum(lax.dot_general(part, pick, NN, preferred_element_type=F32)
               for part in (halves[0], halves[1], rest.astype(BF16)))
    coeffs_ref[...] = dot3(inverse, split(mine), NN)[:, 0:width]


def finish(packed, matrix, sketch, scale, width):
    vmem = pl.BlockSpec(memory_space=pltpu.VMEM)
    return pl.pallas_call(
        functools.partial(finish_kernel, scale),
        out_shape=(jax.ShapeDtypeStruct((256, 256), F32), jax.ShapeDtypeStruct((256, width), F32)),
        in_specs=[vmem] * 3,
        out_specs=(vmem, vmem),
        scratch_shapes=[
            pltpu.VMEM((768, 768), BF16),
            pltpu.VMEM((768, 768), BF16),
            pltpu.VMEM((256, 256), F32),
            pltpu.VMEM((256, 256), F32),
        ],
        compiler_params=pltpu.CompilerParams(vmem_limit_bytes=40 * 1024 * 1024),
        name="finish",
    )(packed, matrix, sketch)


def shards(matrix, sketch):
    parts = lax.axis_size("rows") * lax.axis_size("grp")
    packed = reduced_gram(matrix)
    scale = float((matrix.shape[0] * parts) ** 0.5)
    return finish(packed, matrix, sketch, scale, matrix.shape[1] // lax.axis_size("rows"))


def solution(mesh):
    return jax.shard_map(
        shards,
        mesh=mesh,
        in_specs=(P(("rows", "grp"), None), P()),
        out_specs=(P(("rows", "grp"), None), P(None, "rows")),
        check_vma=False,
    )
```

time: 900 us -> 71.5 us (0.08)
  waiting for transfers between devices: 811 us -> 0 us
  Pallas kernels: 0 us -> 68.9 us
  other arithmetic: 53.8 us -> 0 us
  between operations: 15.2 us -> 0.65 us
  matrix products: 10.4 us -> 0 us
    psum x3 -> x0, waiting for transfers between devices: 811 us -> none  [the longest x1 278 us: shards(): power = lax.psum(mult(matrix.T, proj), ('rows', 'grp'))]
    pallas_call x0 -> x2, Pallas kernels: none -> 68.9 us  [the longest x1 54.5 us: reduced_gram(): pl.pallas_call(reduce_kernel, out_shape=jax.ShapeDtypeStruct((2, NX, LIVE...]
    another operation x9 -> x0, other arithmetic: 53.7 us -> none  [the longest x6 34 us: shards(): lower = jnp.linalg.cholesky(gram)]
    dot_general x5 -> x0, matrix products: 9.06 us -> none  [mult(): jnp.dot(left, right, precision=lax.Precision.HIGHEST, preferred_element_t...]
  transfers between devices with their start and end apart: 3 -> 0, of which waited for: 3 -> 0; matrix products, arithmetic and copies ran while one was open for 0% -> 0% of each run, Pallas kernels for 0% -> 0%
where the time goes in v1:
time: 71.5 us; the launch traced here: 71.4 us
  Pallas kernels  68.9 us (96%)
  local copies, waits for them, and re-layouts  1.82 us (3%)
    pallas_call x1, Pallas kernels, reduced_gram(): pl.pallas_call(reduce_kernel, out_shape=jax.ShapeDtypeStruct((2, NX, LIVE...  54.5 us
    pallas_call x1, Pallas kernels, finish(): pl.pallas_call(functools.partial(finish_kernel, scale), out_shape=(jax.Sh...  14.4 us

profile of v1, /device:TPU:1, one launch (start us, length us, event | category | flops | bytes accessed | tf_op | source)
XLA Modules:
  0.0 71.4 jit_solution(15718082929673414772)
XLA Ops:
  0.6 0.0 copy-start
  0.6 1.1 %copy-done = f32[256,768]{1,0:T(8,128)S(1)} copy-done((f32[256,768]{1,0:T(8,128)S(1)}, f32[256,768]{1,0:T(8,128)}, u32[]{:S(2)}) %copy-start) | copy-done | bytes 786456
  1.8 0.0 copy-start.1
  1.8 54.5 %reduce_gram.1.packed = f32[2,4,336,128]{3,2,1,0:T(8,128)S(1)} custom-call(f32[256,768]{1,0:T(8,128)S(1)} %copy-done), custom_call_target="tpu_custom_call" | custom-call | tf_op jit(solution)/shard_map/reduce_gram/pallas_call | solution.py:196
  56.3 0.0 copy-done.1
  56.3 14.4 %finish.1 = (f32[256,256]{1,0:T(8,128)}, f32[256,12]{1,0:T(8,128)S(1)}) custom-call(f32[2,4,336,128]{3,2,1,0:T(8,128)S(1)} %reduce_gram.1.packed, f32[256,768]{1,0:T(8,128)S(1)} %copy-done, f32[768,256]{1,0:T(8,128)S(1)} %copy-done.1), custom_call_target="tpu_custom_call" | custom-call | tf_op jit(solution)/shard_map/finish/pallas_call | solution.py:321
  70.7 0.7 copy.4
Async XLA Ops:
  0.6 1.1 %copy-start = (f32[256,768]{1,0:T(8,128)S(1)}, f32[256,768]{1,0:T(8,128)}, u32[]{:S(2)}) copy-start(f32[256,768]{1,0:T(8,128)} %a_ref.1) | copy-start | bytes 2359300
  1.8 54.5 %copy-start.1 = (f32[768,256]{1,0:T(8,128)S(1)}, f32[768,256]{1,0:T(8,128)}, u32[]{:S(2)}) copy-start(f32[768,256]{1,0:T(8,128)} %s_ref.1) | copy-start | bytes 2359300

commit v2 on v1

v2 whole, which is shorter than its diff:
```python
import functools
import jax
import jax.numpy as jnp
from jax import lax
from jax.experimental import pallas as pl
from jax.experimental.pallas import tpu as pltpu
from jax.sharding import PartitionSpec as P

MESH = pl.DeviceIdType.MESH
F32 = jnp.float32
BF16 = jnp.bfloat16
NX, NY, NZ = 4, 8, 8
BLOCKS = [(i, j) for i in range(6) for j in range(i, 6)]
LIVE = 336
HELD = 384
PIECE = 24


def split(v):
    high = v.astype(BF16)
    return high, (v - high.astype(F32)).astype(BF16)


NN = (((1,), (0,)), ((), ()))
NT = (((1,), (1,)), ((), ()))
TN = (((0,), (0,)), ((), ()))


def dot3(left, right, dims):
    def one(a, b):
        return lax.dot_general(a, b, dims, preferred_element_type=F32)
    return one(left[0], right[1]) + one(left[1], right[0]) + one(left[0], right[0])


def place(tile):
    share, row = divmod(tile, LIVE // 8)
    return share // NX, share % NX, row * 8


def store_block(part, index, value):
    for t in range(16):
        core, x, row = place(index * 16 + t)
        part[core, x, row:row + 8, :] = value[8 * t:8 * t + 8, :]


PARTS = (pl.ds(0, HELD // 2), pl.ds(HELD // 2, LIVE - HELD // 2))


def reduce_kernel(a_hbm, high, low, a_own, part, sib_in, x_in, acc, z_in, y_in, zy, yz, gath, load_sem,
                  sib_s, sib_r, x_s, x_r, z_s, z_r, y_s, y_r, zy_s, zy_r, yz_s, yz_r,
                  zg_s, zg_r, yg_s, yg_r, xg_s, xg_r, fw_s, fw_r):
    r = lax.axis_index("rows")
    y = lax.axis_index("grp")
    x, z, c = r // 16, lax.rem(r // 2, 8), lax.rem(r, 2)

    def dev(xx, yy, zz, cc):
        return ((xx * NZ + zz) * 2 + cc, yy)

    def other(axis, k):
        if axis == "x":
            return lax.rem(x + k, NX), dev(lax.rem(x + k, NX), y, z, c)
        if axis == "y":
            return lax.rem(y + k, NY), dev(x, lax.rem(y + k, NY), z, c)
        return lax.rem(z + k, NZ), dev(x, y, lax.rem(z + k, NZ), c)

    sibling = dev(x, y, z, 1 - c)
    load = pltpu.make_async_copy(a_hbm, a_own, load_sem)
    load.start()
    barrier = pltpu.get_barrier_semaphore()
    for axis, n in (("x", NX), ("y", NY), ("z", NZ)):
        for k in range(1, n):
            pl.semaphore_signal(barrier, inc=1, device_id=other(axis, k)[1], device_id_type=MESH)
    pl.semaphore_signal(barrier, inc=1, device_id=sibling, device_id_type=MESH)

    def copy(src, dst, s, rr, to=sibling):
        return pltpu.make_async_remote_copy(src_ref=src, dst_ref=dst, send_sem=s, recv_sem=rr,
                                            device_id=to, device_id_type=MESH)

    sent = []

    def send(*args):
        d = copy(*args)
        d.start()
        sent.append(d)

    load.wait()
    halves = split(a_own[...])
    for i in range(6):
        lo = 128 * i
        strip = dot3((halves[0][:, lo:lo + 128], halves[1][:, lo:lo + 128]), (halves[0][:, lo:], halves[1][:, lo:]), TN)
        for j in range(i, 6):
            store_block(part, BLOCKS.index((i, j)), strip[:, 128 * j - lo:128 * j - lo + 128])

    pl.semaphore_wait(barrier, 1 + (NX - 1) + (NY - 1) + (NZ - 1))

    order = (2, 1, 3, 0)
    quarters = [lax.rem(x + k, NX) for k in order]
    for h, rows in enumerate(PARTS):
        for xx in quarters:
            send(part.at[1 - c, xx, rows], sib_in.at[xx, rows], sib_s.at[h, xx], sib_r.at[h, xx], sibling)
    for h, rows in enumerate(PARTS):
        for k, xx in zip(order, quarters):
            copy(part.at[1 - c, xx, rows], sib_in.at[xx, rows], sib_s.at[h, xx], sib_r.at[h, xx]).wait_recv()
            part[c, xx, rows, :] = part[c, xx, rows, :] + sib_in[xx, rows, :]
            if k:
                send(part.at[c, xx, rows], x_in.at[k - 1, rows], x_s.at[h, k - 1], x_r.at[h, k - 1], other("x", k)[1])
    acc[LIVE:HELD, :] = jnp.zeros((HELD - LIVE, 128), F32)

    def piece(half, owner):
        return pl.ds(pl.multiple_of(half * (HELD // 2) + owner * PIECE, 8), PIECE)

    along = (("z", z, z_in, z_s, z_r), ("y", y, y_in, y_s, y_r))
    for h, (axis, me, box, ss, rs) in enumerate(along):
        rows = PARTS[h]
        for k in (1, 3, 2):
            copy(part.at[c, x, rows], x_in.at[k - 1, rows], x_s.at[h, k - 1], x_r.at[h, k - 1]).wait_recv()
        acc[rows, :] = part[c, x, rows, :] + (x_in[0, rows, :] + x_in[1, rows, :] + x_in[2, rows, :])
        for k in (4, 3, 5, 2, 6, 1, 7):
            to, device = other(axis, k)
            send(acc.at[piece(h, to)], box.at[k - 1], ss.at[k - 1], rs.at[k - 1], device)
    cross = (("y", y, zy, zy_s, zy_r), ("z", z, yz, yz_s, yz_r))
    for h, (axis, me, box, ss, rs) in enumerate(along):
        for k in range(1, 8):
            copy(acc.at[piece(h, me)], box.at[k - 1], ss.at[k - 1], rs.at[k - 1]).wait_recv()
        total = acc[piece(h, me), :]
        for k in range(1, 8):
            total += box[k - 1]
        axis, me, box, ss, rs = cross[h]
        box[me] = total
        for k in (4, 3, 5, 2, 6, 1, 7):
            send(box.at[me], box.at[me], ss.at[k - 1], rs.at[me], other(axis, k)[1])
    mine = gath.at[c, x]
    back = (("z", z, zg_s, zg_r), ("y", y, yg_s, yg_r))
    for h, (axis, me, box, ss, rs) in enumerate(cross):
        for k in range(1, 8):
            at, _ = other(axis, k)
            copy(box.at[at], box.at[at], ss.at[k - 1], rs.at[at]).wait_recv()
        total = box[0]
        for k in range(1, 8):
            total += box[k]
        axis, me, ss, rs = back[h]
        gath[c, x, piece(h, me), :] = total
        for k in (4, 3, 5, 2, 6, 1, 7):
            send(mine.at[piece(h, me)], mine.at[piece(h, me)], ss.at[k - 1], rs.at[me], other(axis, k)[1])
    def halve(core, xx, h):
        share = core * NX + xx
        for n in range(PARTS[h].size // 16):
            row = PARTS[h].start + 16 * n
            high[share, row:row + 16, :], low[share, row:row + 16, :] = split(gath[core, xx, row:row + 16, :])

    for h, (axis, me, ss, rs) in enumerate(back):
        for k in range(1, 8):
            at, _ = other(axis, k)
            copy(mine.at[piece(h, at)], mine.at[piece(h, at)], ss.at[k - 1], rs.at[at]).wait_recv()
        rows = PARTS[h]
        quarter = gath.at[c, x, rows]
        for k in (2, 1, 3):
            send(quarter, quarter, xg_s.at[h, k - 1], xg_r.at[h, x], other("x", k)[1])
        send(quarter, quarter, fw_s.at[h, x], fw_r.at[h, x], sibling)
        halve(c, x, h)
    for h, rows in enumerate(PARTS):
        for k in (1, 3, 2):
            xx, _ = other("x", k)
            came = gath.at[c, xx, rows]
            copy(came, came, xg_s.at[h, k - 1], xg_r.at[h, xx]).wait_recv()
            send(came, came, fw_s.at[h, xx], fw_r.at[h, xx], sibling)
            halve(c, xx, h)
    for h, rows in enumerate(PARTS):
        for k in (0, 1, 3, 2):
            xx, _ = other("x", k)
            came = gath.at[1 - c, xx, rows]
            copy(came, came, fw_s.at[h, xx], fw_r.at[h, xx]).wait_recv()
            halve(1 - c, xx, h)
    for d in sent:
        d.wait_send()


def dma(*shape):
    return pltpu.SemaphoreType.DMA(shape)


def reduced_gram(matrix):
    rows, cols = matrix.shape
    vmem = pl.BlockSpec(memory_space=pltpu.VMEM)
    return pl.pallas_call(
        reduce_kernel,
        out_shape=[jax.ShapeDtypeStruct((2 * NX, LIVE, 128), BF16)] * 2,
        in_specs=[pl.BlockSpec(memory_space=pltpu.HBM)],
        out_specs=[vmem] * 2,
        scratch_shapes=[
            pltpu.VMEM((rows, cols), F32),
            pltpu.VMEM((2, NX, HELD, 128), F32),
            pltpu.VMEM((NX, LIVE, 128), F32),
            pltpu.VMEM((NX - 1, LIVE, 128), F32),
            pltpu.VMEM((HELD, 128), F32),
            pltpu.VMEM((7, PIECE, 128), F32),
            pltpu.VMEM((7, PIECE, 128), F32),
            pltpu.VMEM((8, PIECE, 128), F32),
            pltpu.VMEM((8, PIECE, 128), F32),
            pltpu.VMEM((2, NX, HELD, 128), F32),
            pltpu.SemaphoreType.DMA,
            dma(2, 4), dma(2, 4), dma(2, 3), dma(2, 3), dma(7), dma(7), dma(7), dma(7),
            dma(7), dma(8), dma(7), dma(8), dma(7), dma(8), dma(7), dma(8),
            dma(2, 3), dma(2, 4), dma(2, 4), dma(2, 4),
        ],
        compiler_params=pltpu.CompilerParams(collective_id=0, has_side_effects=True,
                                             vmem_limit_bytes=40 * 1024 * 1024),
        name="reduce_gram",
    )(matrix)


def panel_inverse_8(d, nb):
    n8 = nb // 8
    eye = (lax.broadcasted_iota(jnp.int32, (nb, nb), 0) == lax.broadcasted_iota(jnp.int32, (nb, nb), 1)).astype(F32)
    w = jnp.concatenate([d, eye], 1)
    groups = [w[8 * g:8 * g + 8, :] for g in range(n8)]
    sub = lax.broadcasted_iota(jnp.int32, (8, 128), 0)
    out = [None] * n8
    for g in range(n8):
        cols = {h: [jnp.broadcast_to(groups[h][:, 8 * g + k:8 * g + k + 1], (8, 128)) for k in range(8)] for h in range(g, n8)}
        pivots = []
        for k in range(8):
            row = jnp.broadcast_to(groups[g][k:k + 1, :], (8, 128))
            rows = {m: jnp.broadcast_to(cols[g][m][k:k + 1, :], (8, 128)) for m in range(k, 8)}
            inv = 1.0 / rows[k]
            pivots.append(rows[k])
            q = row * inv
            qs = {m: rows[m] * inv for m in range(k + 1, 8)}
            for h in range(g, n8):
                c = cols[h][k]
                if h == g:
                    c = jnp.where(sub > k, c, 0.0)
                groups[h] = groups[h] - c * q
                for m in range(k + 1, 8):
                    cols[h][m] = cols[h][m] - c * qs[m]
        dia = pivots[7]
        for k in range(7):
            dia = jnp.where(sub == k, pivots[k], dia)
        out[g] = groups[g][:, nb:] * lax.rsqrt(dia)[:, nb:]
    return jnp.concatenate(out, 0)


def cholesky_inverse(gram, linv, nb, panel):
    n = gram.shape[0]
    linv[...] = jnp.zeros((n, n), F32)
    for b in range(n // nb):
        lo, hi = b * nb, (b + 1) * nb
        x = panel(gram[lo:hi, lo:hi], nb)
        xs = split(x)
        if b:
            done = dot3(xs, split(linv[lo:hi, 0:lo]), NN)
            linv[lo:hi, 0:lo] = done
        linv[lo:hi, lo:hi] = x
        if hi < n:
            u = split(dot3(xs, split(gram[lo:hi, hi:n]), NN))
            gram[hi:n, hi:n] = gram[hi:n, hi:n] - dot3(u, u, TN)
            linv[hi:n, 0:hi] = linv[hi:n, 0:hi] - dot3(u, split(linv[lo:hi, 0:hi]), TN)


def upper(ref, i, j):
    at = 128 * BLOCKS.index((i, j))
    return ref[at:at + 128, :]


def gram_strips(ref, corners):
    strips = []
    for s in range(3):
        p, q = 2 * s, 2 * s + 1
        above = [jnp.concatenate([upper(ref, i, p), upper(ref, i, q)], 1) for i in range(q)]
        above.append(jnp.concatenate([corners[s], upper(ref, q, q)], 1))
        right = None
        if s < 2:
            right = jnp.concatenate([jnp.concatenate([upper(ref, i, j) for j in range(q + 1, 6)], 1) for i in (p, q)], 0)
        strips.append((jnp.concatenate(above, 0), right))
    return strips


def times_gram(left, high, low):
    out = []
    for s in range(3):
        hi = 256 * s + 256
        strip = dot3((left[0][:, :hi], left[1][:, :hi]), (high[s][0], low[s][0]), NN)
        if s < 2:
            strip += dot3((left[0][:, hi:], left[1][:, hi:]), (high[s][1], low[s][1]), NT)
        out.append(strip)
    return jnp.concatenate(out, 1)


def finish_kernel(scale, g_high, g_low, matrix, sketch, basis_ref, coeffs_ref, gram, linv):
    r = lax.axis_index("rows")
    high, low = (gram_strips(ref, [upper(ref, 2 * s, 2 * s + 1).T for s in range(3)]) for ref in (g_high, g_low))
    power = split(times_gram(split(sketch[...].T), high, low))
    ranged = times_gram(power, high, low)
    halves = split(ranged)
    gram[...] = dot3(halves, power, NT)
    cholesky_inverse(gram, linv, 64, panel_inverse_8)
    inverse = split(linv[...])
    factor = split(dot3(inverse, power, NN))
    basis_ref[...] = dot3(split(matrix[...]), factor, NT) * scale
    width = coeffs_ref.shape[0]
    row = lax.broadcasted_iota(jnp.int32, (128, 768), 0)
    col = lax.broadcasted_iota(jnp.int32, (128, 768), 1)
    pick = jnp.where(col == row + r * width, 1.0, 0.0).astype(BF16)
    rest = (ranged - halves[0].astype(F32)) - halves[1].astype(F32)
    mine = sum(lax.dot_general(pick, part, NT, preferred_element_type=F32)
               for part in (halves[0], halves[1], rest.astype(BF16)))
    coeffs_ref[...] = dot3(split(mine), inverse, NT)[0:width, :]


def finish(operands, scale, width):
    vmem = pl.BlockSpec(memory_space=pltpu.VMEM)
    return pl.pallas_call(
        functools.partial(finish_kernel, scale),
        out_shape=(jax.ShapeDtypeStruct((256, 256), F32), jax.ShapeDtypeStruct((width, 256), F32)),
        in_specs=[vmem] * 4,
        out_specs=(vmem, vmem),
        scratch_shapes=[pltpu.VMEM((256, 256), F32), pltpu.VMEM((256, 256), F32)],
        compiler_params=pltpu.CompilerParams(vmem_limit_bytes=40 * 1024 * 1024),
        name="finish",
    )(*operands)


def shards(matrix, sketch):
    parts = lax.axis_size("rows") * lax.axis_size("grp")
    high, low = reduced_gram(matrix)
    scale = float((matrix.shape[0] * parts) ** 0.5)
    width = matrix.shape[1] // lax.axis_size("rows")
    basis, coeffs = finish((high.reshape(-1, 128), low.reshape(-1, 128), matrix, sketch), scale, width)
    return basis, coeffs.T


def solution(mesh):
    return jax.shard_map(
        shards,
        mesh=mesh,
        in_specs=(P(("rows", "grp"), None), P()),
        out_specs=(P(("rows", "grp"), None), P(None, "rows")),
        check_vma=False,
    )
```

time: 71.5 us -> 65.8 us (0.920)
  Pallas kernels: 68.9 us -> 63.9 us
    pallas_call x1, Pallas kernels: 54.5 us -> 49.5 us  [reduced_gram(): pl.pallas_call(reduce_kernel, out_shape=[jax.ShapeDtypeStruct((2 * NX, LI...]
where the time goes in v2:
time: 65.8 us; the launch traced here: 65.7 us
  Pallas kernels  63.9 us (97%)
  local copies, waits for them, and re-layouts  1.13 us (2%)
    pallas_call x1, Pallas kernels, reduced_gram(): pl.pallas_call(reduce_kernel, out_shape=[jax.ShapeDtypeStruct((2 * NX, LI...  49.5 us
    pallas_call x1, Pallas kernels, finish(): pl.pallas_call(functools.partial(finish_kernel, scale), out_shape=(jax.Sh...  14.4 us

profile of v2, /device:TPU:1, one launch (start us, length us, event | category | flops | bytes accessed | tf_op | source)
XLA Modules:
  0.0 65.7 jit_solution(1241798127532191273)
XLA Ops:
  0.6 0.0 copy-start
  0.6 1.1 %copy-done = f32[256,768]{1,0:T(8,128)S(1)} copy-done((f32[256,768]{1,0:T(8,128)S(1)}, f32[256,768]{1,0:T(8,128)}, u32[]{:S(2)}) %copy-start) | copy-done | bytes 786456
  1.8 0.0 copy-start.1
  1.8 49.5 %reduce_gram.1 = (bf16[8,336,128]{2,1,0:T(8,128)(2,1)S(1)}, bf16[8,336,128]{2,1,0:T(8,128)(2,1)S(1)}) custom-call(f32[256,768]{1,0:T(8,128)S(1)} %copy-done), custom_call_target="tpu_custom_call" | custom-call | tf_op jit(solution)/shard_map/reduce_gram/pallas_call | solution.py:185
  51.2 0.0 copy-done.1
  51.3 14.4 %finish.1 = (f32[256,256]{1,0:T(8,128)}, f32[12,256]{1,0:T(8,128)}) custom-call(bf16[2688,128]{1,0:T(8,128)(2,1)S(1)} %bitcast.3, bf16[2688,128]{1,0:T(8,128)(2,1)S(1)} %bitcast.4, f32[256,768]{1,0:T(8,128)S(1)} %copy-done, f32[768,256]{1,0:T(8,128)S(1)} %copy-done.1), custom_call_target="tpu_custom_call" | custom-call | tf_op jit(solution)/shard_map/finish/pallas_call | solution.py:312
Async XLA Ops:
  0.6 1.1 %copy-start = (f32[256,768]{1,0:T(8,128)S(1)}, f32[256,768]{1,0:T(8,128)}, u32[]{:S(2)}) copy-start(f32[256,768]{1,0:T(8,128)} %matrix.1) | copy-start | bytes 2359300
  1.8 49.5 %copy-start.1 = (f32[768,256]{1,0:T(8,128)S(1)}, f32[768,256]{1,0:T(8,128)}, u32[]{:S(2)}) copy-start(f32[768,256]{1,0:T(8,128)} %sketch.1) | copy-start | bytes 2359300

commit v3 on v2

--- a/solution.py
+++ b/solution.py
@@ -44,10 +44,11 @@
 
 
 PARTS = (pl.ds(0, HELD // 2), pl.ds(HELD // 2, LIVE - HELD // 2))
-
-
-def reduce_kernel(a_hbm, high, low, a_own, part, sib_in, x_in, acc, z_in, y_in, zy, yz, gath, load_sem,
-                  sib_s, sib_r, x_s, x_r, z_s, z_r, y_s, y_r, zy_s, zy_r, yz_s, yz_r,
+SUBS = tuple((pl.ds(p.start, p.size // 2), pl.ds(p.start + p.size // 2, p.size // 2)) for p in PARTS)
+
+
+def reduce_kernel(a_hbm, s_hbm, high, low, st_high, st_low, a_own, s_own, part, sib_in, relay_in, x_in, acc, z_in, y_in, zy, yz, gath, load_sem,
+                  sib_s, sib_r, rl_s, rl_r, x_s, x_r, z_s, z_r, y_s, y_r, zy_s, zy_r, yz_s, yz_r,
                   zg_s, zg_r, yg_s, yg_r, xg_s, xg_r, fw_s, fw_r):
     r = lax.axis_index("rows")
     y = lax.axis_index("grp")
@@ -64,13 +65,15 @@
         return lax.rem(z + k, NZ), dev(x, y, lax.rem(z + k, NZ), c)
 
     sibling = dev(x, y, z, 1 - c)
-    load = pltpu.make_async_copy(a_hbm, a_own, load_sem)
+    load = pltpu.make_async_copy(a_hbm, a_own, load_sem.at[0])
     load.start()
     barrier = pltpu.get_barrier_semaphore()
     for axis, n in (("x", NX), ("y", NY), ("z", NZ)):
         for k in range(1, n):
             pl.semaphore_signal(barrier, inc=1, device_id=other(axis, k)[1], device_id_type=MESH)
     pl.semaphore_signal(barrier, inc=1, device_id=sibling, device_id_type=MESH)
+    load_s = pltpu.make_async_copy(s_hbm, s_own, load_sem.at[1])
+    load_s.start()
 
     def copy(src, dst, s, rr, to=sibling):
         return pltpu.make_async_remote_copy(src_ref=src, dst_ref=dst, send_sem=s, recv_sem=rr,
@@ -93,17 +96,43 @@
 
     pl.semaphore_wait(barrier, 1 + (NX - 1) + (NY - 1) + (NZ - 1))
 
-    order = (2, 1, 3, 0)
-    quarters = [lax.rem(x + k, NX) for k in order]
+    right, to_right = other("x", 1)
+    left, to_left = other("x", 3)
+    across, _ = other("x", 2)
     for h, rows in enumerate(PARTS):
-        for xx in quarters:
+        for xx in (across, right, left, x):
             send(part.at[1 - c, xx, rows], sib_in.at[xx, rows], sib_s.at[h, xx], sib_r.at[h, xx], sibling)
-    for h, rows in enumerate(PARTS):
-        for k, xx in zip(order, quarters):
-            copy(part.at[1 - c, xx, rows], sib_in.at[xx, rows], sib_s.at[h, xx], sib_r.at[h, xx]).wait_recv()
-            part[c, xx, rows, :] = part[c, xx, rows, :] + sib_in[xx, rows, :]
-            if k:
-                send(part.at[c, xx, rows], x_in.at[k - 1, rows], x_s.at[h, k - 1], x_r.at[h, k - 1], other("x", k)[1])
+
+    def add_sibling(h, xx):
+        rows = PARTS[h]
+        copy(part.at[1 - c, xx, rows], sib_in.at[xx, rows], sib_s.at[h, xx], sib_r.at[h, xx]).wait_recv()
+        part[c, xx, rows, :] = part[c, xx, rows, :] + sib_in[xx, rows, :]
+
+    def relay(h, n, to=sibling):
+        rows = SUBS[h][n]
+        return part.at[c, across, rows], relay_in.at[rows], rl_s.at[h, n], rl_r.at[h, n], to
+
+    def one_step(h, way, n, to=sibling):
+        rows = SUBS[h][n]
+        return part.at[c, (right, left)[way], rows], x_in.at[way, rows], x_s.at[h, way, n], x_r.at[h, way, n], to
+
+    for h in range(2):
+        add_sibling(h, across)
+        send(*relay(h, 0, to_right))
+        send(*relay(h, 1, to_left))
+        add_sibling(h, right)
+        send(*one_step(h, 0, 1, to_right))
+        add_sibling(h, left)
+        send(*one_step(h, 1, 0, to_left))
+        add_sibling(h, x)
+    for h in range(2):
+        for n, (xx, to) in enumerate(((right, to_right), (left, to_left))):
+            rows = SUBS[h][n]
+            copy(*relay(h, n)).wait_recv()
+            part[c, xx, rows, :] = part[c, xx, rows, :] + relay_in[rows, :]
+            send(*one_step(h, n, n, to))
+    load_s.wait()
+    st_high[...], st_low[...] = split(s_own[...].T)
     acc[LIVE:HELD, :] = jnp.zeros((HELD - LIVE, 128), F32)
 
     def piece(half, owner):
@@ -112,9 +141,9 @@
     along = (("z", z, z_in, z_s, z_r), ("y", y, y_in, y_s, y_r))
     for h, (axis, me, box, ss, rs) in enumerate(along):
         rows = PARTS[h]
-        for k in (1, 3, 2):
-            copy(part.at[c, x, rows], x_in.at[k - 1, rows], x_s.at[h, k - 1], x_r.at[h, k - 1]).wait_recv()
-        acc[rows, :] = part[c, x, rows, :] + (x_in[0, rows, :] + x_in[1, rows, :] + x_in[2, rows, :])
+        for way, n in ((0, 1), (1, 0), (0, 0), (1, 1)):
+            copy(*one_step(h, way, n)).wait_recv()
+        acc[rows, :] = part[c, x, rows, :] + (x_in[0, rows, :] + x_in[1, rows, :])
         for k in (4, 3, 5, 2, 6, 1, 7):
             to, device = other(axis, k)
             send(acc.at[piece(h, to)], box.at[k - 1], ss.at[k - 1], rs.at[k - 1], device)
@@ -148,26 +177,27 @@
             row = PARTS[h].start + 16 * n
             high[share, row:row + 16, :], low[share, row:row + 16, :] = split(gath[core, xx, row:row + 16, :])
 
+    def whole(h, xx):
+        ref = gath.at[c, xx, PARTS[h]]
+        return ref, ref, fw_s.at[h, xx], fw_r.at[h, xx], sibling
+
     for h, (axis, me, ss, rs) in enumerate(back):
         for k in range(1, 8):
             at, _ = other(axis, k)
             copy(mine.at[piece(h, at)], mine.at[piece(h, at)], ss.at[k - 1], rs.at[at]).wait_recv()
         rows = PARTS[h]
-        quarter = gath.at[c, x, rows]
         for k in (2, 1, 3):
-            send(quarter, quarter, xg_s.at[h, k - 1], xg_r.at[h, x], other("x", k)[1])
-        send(quarter, quarter, fw_s.at[h, x], fw_r.at[h, x], sibling)
+            send(mine.at[rows], mine.at[rows], xg_s.at[h, k - 1], xg_r.at[h, x], other("x", k)[1])
+        send(*whole(h, x))
         halve(c, x, h)
     for h, rows in enumerate(PARTS):
-        for k in (1, 3, 2):
-            xx, _ = other("x", k)
+        for xx in (left, right, across):
             came = gath.at[c, xx, rows]
-            copy(came, came, xg_s.at[h, k - 1], xg_r.at[h, xx]).wait_recv()
-            send(came, came, fw_s.at[h, xx], fw_r.at[h, xx], sibling)
+            copy(came, came, xg_s.at[h, 0], xg_r.at[h, xx]).wait_recv()
+            send(*whole(h, xx))
             halve(c, xx, h)
     for h, rows in enumerate(PARTS):
-        for k in (0, 1, 3, 2):
-            xx, _ = other("x", k)
+        for xx in (x, left, right, across):
             came = gath.at[1 - c, xx, rows]
             copy(came, came, fw_s.at[h, xx], fw_r.at[h, xx]).wait_recv()
             halve(1 - c, xx, h)
@@ -179,82 +209,109 @@
     return pltpu.SemaphoreType.DMA(shape)
 
 
-def reduced_gram(matrix):
+def reduced_gram(matrix, sketch):
     rows, cols = matrix.shape
     vmem = pl.BlockSpec(memory_space=pltpu.VMEM)
     return pl.pallas_call(
         reduce_kernel,
-        out_shape=[jax.ShapeDtypeStruct((2 * NX, LIVE, 128), BF16)] * 2,
-        in_specs=[pl.BlockSpec(memory_space=pltpu.HBM)],
-        out_specs=[vmem] * 2,
+        out_shape=[jax.ShapeDtypeStruct((2 * NX, LIVE, 128), BF16)] * 2 + [jax.ShapeDtypeStruct(sketch.shape[::-1], BF16)] * 2,
+        in_specs=[pl.BlockSpec(memory_space=pltpu.HBM)] * 2,
+        out_specs=[vmem] * 4,
         scratch_shapes=[
             pltpu.VMEM((rows, cols), F32),
+            pltpu.VMEM(sketch.shape, F32),
             pltpu.VMEM((2, NX, HELD, 128), F32),
             pltpu.VMEM((NX, LIVE, 128), F32),
-            pltpu.VMEM((NX - 1, LIVE, 128), F32),
+            pltpu.VMEM((LIVE, 128), F32),
+            pltpu.VMEM((2, LIVE, 128), F32),
             pltpu.VMEM((HELD, 128), F32),
             pltpu.VMEM((7, PIECE, 128), F32),
             pltpu.VMEM((7, PIECE, 128), F32),
             pltpu.VMEM((8, PIECE, 128), F32),
             pltpu.VMEM((8, PIECE, 128), F32),
             pltpu.VMEM((2, NX, HELD, 128), F32),
-            pltpu.SemaphoreType.DMA,
-            dma(2, 4), dma(2, 4), dma(2, 3), dma(2, 3), dma(7), dma(7), dma(7), dma(7),
+            dma(2),
+            dma(2, 4), dma(2, 4), dma(2, 2), dma(2, 2), dma(2, 2, 2), dma(2, 2, 2), dma(7), dma(7), dma(7), dma(7),
             dma(7), dma(8), dma(7), dma(8), dma(7), dma(8), dma(7), dma(8),
             dma(2, 3), dma(2, 4), dma(2, 4), dma(2, 4),
         ],
         compiler_params=pltpu.CompilerParams(collective_id=0, has_side_effects=True,
-                                             vmem_limit_bytes=40 * 1024 * 1024),
+                                             vmem_limit_bytes=103 * 512 * 1024),
         name="reduce_gram",
-    )(matrix)
-
-
-def panel_inverse_8(d, nb):
-    n8 = nb // 8
-    eye = (lax.broadcasted_iota(jnp.int32, (nb, nb), 0) == lax.broadcasted_iota(jnp.int32, (nb, nb), 1)).astype(F32)
-    w = jnp.concatenate([d, eye], 1)
-    groups = [w[8 * g:8 * g + 8, :] for g in range(n8)]
+    )(matrix, sketch)
+
+
+NB = 64
+
+
+def spread(v):
+    return jnp.broadcast_to(v, (8, 128))
+
+
+def eliminate(w, at):
+    n8 = w.shape[0] // 8
+    lanes = range(w.shape[1] // 128)
+    groups = [[w[8 * g:8 * g + 8, 128 * v:128 * v + 128] for v in lanes] for g in range(n8)]
     sub = lax.broadcasted_iota(jnp.int32, (8, 128), 0)
-    out = [None] * n8
+    out = []
     for g in range(n8):
-        cols = {h: [jnp.broadcast_to(groups[h][:, 8 * g + k:8 * g + k + 1], (8, 128)) for k in range(8)] for h in range(g, n8)}
-        pivots = []
-        for k in range(8):
-            row = jnp.broadcast_to(groups[g][k:k + 1, :], (8, 128))
-            rows = {m: jnp.broadcast_to(cols[g][m][k:k + 1, :], (8, 128)) for m in range(k, 8)}
-            inv = 1.0 / rows[k]
-            pivots.append(rows[k])
-            q = row * inv
-            qs = {m: rows[m] * inv for m in range(k + 1, 8)}
+        base = at + 8 * g
+        cols = {h: [spread(groups[h][0][:, base + k:base + k + 1]) for k in range(8)] for h in range(g, n8)}
+        pairs = []
+        for k in range(0, 8, 2):
+            e0 = {m: spread(cols[g][m][k:k + 1, :]) for m in range(k, 8)}
+            e1 = {m: spread(cols[g][m][k + 1:k + 2, :]) for m in range(k + 1, 8)}
+            a, b, c = e0[k], e0[k + 1], e1[k + 1]
+            det = a * c - b * b
+            inv = 1.0 / det
+            pairs.append((a, b, det))
+            v0 = {m: (c * e0[m] - b * e1[m]) * inv for m in range(k + 2, 8)}
+            v1 = {m: (a * e1[m] - b * e0[m]) * inv for m in range(k + 2, 8)}
+            u = []
+            for v in lanes:
+                r0, r1 = spread(groups[g][v][k:k + 1, :]), spread(groups[g][v][k + 1:k + 2, :])
+                u.append(((c * r0 - b * r1) * inv, (a * r1 - b * r0) * inv))
             for h in range(g, n8):
-                c = cols[h][k]
+                c0, c1 = cols[h][k], cols[h][k + 1]
                 if h == g:
-                    c = jnp.where(sub > k, c, 0.0)
-                groups[h] = groups[h] - c * q
-                for m in range(k + 1, 8):
-                    cols[h][m] = cols[h][m] - c * qs[m]
-        dia = pivots[7]
-        for k in range(7):
-            dia = jnp.where(sub == k, pivots[k], dia)
-        out[g] = groups[g][:, nb:] * lax.rsqrt(dia)[:, nb:]
+                    if k == 6:
+                        continue
+                    c0, c1 = jnp.where(sub > k + 1, c0, 0.0), jnp.where(sub > k + 1, c1, 0.0)
+                for m in range(k + 2, 8):
+                    cols[h][m] = cols[h][m] - (c0 * v0[m] + c1 * v1[m])
+                for v in lanes:
+                    groups[h][v] = groups[h][v] - (c0 * u[v][0] + c1 * u[v][1])
+        less, scale = jnp.zeros((8, 128), F32), jnp.zeros((8, 128), F32)
+        for i, (a, b, det) in enumerate(pairs):
+            root = lax.rsqrt(a)
+            less = jnp.where(sub == 2 * i + 1, b / a, less)
+            scale = jnp.where(sub == 2 * i, root, jnp.where(sub == 2 * i + 1, a * root * lax.rsqrt(det), scale))
+        out.append(jnp.concatenate([(p - less * pltpu.roll(p, 1, 0)) * scale for p in groups[g]], 1))
     return jnp.concatenate(out, 0)
 
 
-def cholesky_inverse(gram, linv, nb, panel):
-    n = gram.shape[0]
+def cholesky_inverse(gram, linv, work):
+    n, nb = gram.shape[0], NB
+    same = lax.broadcasted_iota(jnp.int32, (n, n), 0) == lax.broadcasted_iota(jnp.int32, (n, n), 1)
+    diagonal = jnp.where(same, gram, 0.0)
+    unit = lax.rsqrt(jnp.sum(diagonal, 0, keepdims=True))
+    work[:, 0:n] = gram * unit * lax.rsqrt(jnp.sum(diagonal, 1, keepdims=True))
+    work[:, n:] = jnp.where(same, 1.0, 0.0)
     linv[...] = jnp.zeros((n, n), F32)
-    for b in range(n // nb):
-        lo, hi = b * nb, (b + 1) * nb
-        x = panel(gram[lo:hi, lo:hi], nb)
-        xs = split(x)
-        if b:
-            done = dot3(xs, split(linv[lo:hi, 0:lo]), NN)
-            linv[lo:hi, 0:lo] = done
-        linv[lo:hi, lo:hi] = x
+    for lo in range(0, n, nb):
+        hi = lo + nb
+        first, last = lo // 128 * 128, -(-hi // 128) * 128
+        rows = eliminate(jnp.concatenate([work[lo:hi, first:n], work[lo:hi, n:n + last]], 1), lo - first)
+        linv[lo:hi, 0:last] = rows[:, n - first:] * unit[:, 0:last]
         if hi < n:
-            u = split(dot3(xs, split(gram[lo:hi, hi:n]), NN))
-            gram[hi:n, hi:n] = gram[hi:n, hi:n] - dot3(u, u, TN)
-            linv[hi:n, 0:hi] = linv[hi:n, 0:hi] - dot3(u, split(linv[lo:hi, 0:hi]), TN)
+            begin = hi // 128 * 128
+            halves = split(rows)
+            left = tuple(v[:, begin - first:n - first] for v in halves)
+            if begin > first:
+                halves = tuple(v[:, begin - first:] for v in halves)
+            less = dot3(left, halves, TN)[hi - begin:, :]
+            work[hi:n, begin:n] = work[hi:n, begin:n] - less[:, 0:n - begin]
+            work[hi:n, n:n + last] = work[hi:n, n:n + last] - less[:, n - begin:]
 
 
 def upper(ref, i, j):
@@ -286,17 +343,19 @@
     return jnp.concatenate(out, 1)
 
 
-def finish_kernel(scale, g_high, g_low, matrix, sketch, basis_ref, coeffs_ref, gram, linv):
+def finish_kernel(scale, g_high, g_low, st_high, st_low, a_hbm, basis_ref, coeffs_ref, work, linv, a_own, load_sem):
+    load = pltpu.make_async_copy(a_hbm, a_own, load_sem)
+    load.start()
     r = lax.axis_index("rows")
     high, low = (gram_strips(ref, [upper(ref, 2 * s, 2 * s + 1).T for s in range(3)]) for ref in (g_high, g_low))
-    power = split(times_gram(split(sketch[...].T), high, low))
+    power = split(times_gram((st_high[...], st_low[...]), high, low))
     ranged = times_gram(power, high, low)
     halves = split(ranged)
-    gram[...] = dot3(halves, power, NT)
-    cholesky_inverse(gram, linv, 64, panel_inverse_8)
+    cholesky_inverse(dot3(halves, power, NT), linv, work)
     inverse = split(linv[...])
     factor = split(dot3(inverse, power, NN))
-    basis_ref[...] = dot3(split(matrix[...]), factor, NT) * scale
+    load.wait()
+    basis_ref[...] = dot3(split(a_own[...]), factor, NT) * scale
     width = coeffs_ref.shape[0]
     row = lax.broadcasted_iota(jnp.int32, (128, 768), 0)
     col = lax.broadcasted_iota(jnp.int32, (128, 768), 1)
@@ -312,9 +371,14 @@
     return pl.pallas_call(
         functools.partial(finish_kernel, scale),
         out_shape=(jax.ShapeDtypeStruct((256, 256), F32), jax.ShapeDtypeStruct((width, 256), F32)),
-        in_specs=[vmem] * 4,
+        in_specs=[vmem] * 4 + [pl.BlockSpec(memory_space=pltpu.HBM)],
         out_specs=(vmem, vmem),
-        scratch_shapes=[pltpu.VMEM((256, 256), F32), pltpu.VMEM((256, 256), F32)],
+        scratch_shapes=[
+            pltpu.VMEM((256, 512), F32),
+            pltpu.VMEM((256, 256), F32),
+            pltpu.VMEM((256, 768), F32),
+            pltpu.SemaphoreType.DMA,
+        ],
         compiler_params=pltpu.CompilerParams(vmem_limit_bytes=40 * 1024 * 1024),
         name="finish",
     )(*operands)
@@ -322,10 +386,10 @@
 
 def shards(matrix, sketch):
     parts = lax.axis_size("rows") * lax.axis_size("grp")
-    high, low = reduced_gram(matrix)
+    high, low, *rest = reduced_gram(matrix, sketch)
     scale = float((matrix.shape[0] * parts) ** 0.5)
     width = matrix.shape[1] // lax.axis_size("rows")
-    basis, coeffs = finish((high.reshape(-1, 128), low.reshape(-1, 128), matrix, sketch), scale, width)
+    basis, coeffs = finish((high.reshape(-1, 128), low.reshape(-1, 128), *rest, matrix), scale, width)
     return basis, coeffs.T
 
 

time: 65.8 us -> 63.7 us (0.968)
  local copies, waits for them, and re-layouts: 1.13 us -> 0.01 us
  Pallas kernels: 63.9 us -> 62.9 us
    pallas_call x1, Pallas kernels: 14.4 us -> 13.2 us  [finish(): pl.pallas_call(functools.partial(finish_kernel, scale), out_shape=(jax.Sh...]
    unnamed x4 -> x2, local copies, waits for them, and re-layouts: 1.13 us -> 0.01 us
where the time goes in v3:
time: 63.7 us; the launch traced here: 63.6 us
  Pallas kernels  62.9 us (99%)
  between operations  0.65 us (1%)
    pallas_call x1, Pallas kernels, reduced_gram(): pl.pallas_call(reduce_kernel, out_shape=[jax.ShapeDtypeStruct((2 * NX, LI...  49.7 us
    pallas_call x1, Pallas kernels, finish(): pl.pallas_call(functools.partial(finish_kernel, scale), out_shape=(jax.Sh...  13.2 us

profile of v3, /device:TPU:1, one launch (start us, length us, event | category | flops | bytes accessed | tf_op | source)
XLA Modules:
  0.0 63.6 jit_solution(8362744041651274215)
XLA Ops:
  0.6 0.0 copy-start
  0.6 49.7 %reduce_gram.1 = (bf16[8,336,128]{2,1,0:T(8,128)(2,1)S(1)}, bf16[8,336,128]{2,1,0:T(8,128)(2,1)S(1)}, bf16[256,768]{1,0:T(8,128)(2,1)S(1)}, bf16[256,768]{1,0:T(8,128)(2,1)S(1)}) custom-call(f32[256,768]{1,0:T(8,128)} %a_hbm.3, f32[768,256]{1,0:T(8,128)} %s_hbm.1), custom_call_target="tpu_custom_call" | custom-call | tf_op jit(solution)/shard_map/reduce_gram/pallas_call | solution.py:215
  50.4 0.0 copy-done
  50.4 13.2 %finish.1 = (f32[256,256]{1,0:T(8,128)}, f32[12,256]{1,0:T(8,128)}) custom-call(bf16[2688,128]{1,0:T(8,128)(2,1)S(1)} %bitcast.3, bf16[2688,128]{1,0:T(8,128)(2,1)S(1)} %bitcast.4, bf16[256,768]{1,0:T(8,128)(2,1)S(1)} %get-tuple-element.10.st_high, bf16[256,768]{1,0:T(8,128)(2,1)S(1)} %get-tuple-element.11.st_low, f32[256,768]{1,0:T(8,128)S(1)} %copy-done), custom_call_target="tpu_custom_call" | custom-call | tf_op jit(solution)/shard_map/finish/pallas_call | solution.py:371
Async XLA Ops:
  0.6 49.8 %copy-start = (f32[256,768]{1,0:T(8,128)S(1)}, f32[256,768]{1,0:T(8,128)}, u32[]{:S(2)}) copy-start(f32[256,768]{1,0:T(8,128)} %a_hbm.3) | copy-start | bytes 2359300

commit v4 on v3

--- a/solution.py
+++ b/solution.py
@@ -99,9 +99,9 @@
     right, to_right = other("x", 1)
     left, to_left = other("x", 3)
     across, _ = other("x", 2)
-    for h, rows in enumerate(PARTS):
-        for xx in (across, right, left, x):
-            send(part.at[1 - c, xx, rows], sib_in.at[xx, rows], sib_s.at[h, xx], sib_r.at[h, xx], sibling)
+    for h, xx in [(h, xx) for group in ((across,), (right, left), (x,)) for h in range(2) for xx in group]:
+        rows = PARTS[h]
+        send(part.at[1 - c, xx, rows], sib_in.at[xx, rows], sib_s.at[h, xx], sib_r.at[h, xx], sibling)
 
     def add_sibling(h, xx):
         rows = PARTS[h]
@@ -120,10 +120,12 @@
         add_sibling(h, across)
         send(*relay(h, 0, to_right))
         send(*relay(h, 1, to_left))
+    for h in range(2):
         add_sibling(h, right)
         send(*one_step(h, 0, 1, to_right))
         add_sibling(h, left)
         send(*one_step(h, 1, 0, to_left))
+    for h in range(2):
         add_sibling(h, x)
     for h in range(2):
         for n, (xx, to) in enumerate(((right, to_right), (left, to_left))):
@@ -239,9 +241,6 @@
                                              vmem_limit_bytes=103 * 512 * 1024),
         name="reduce_gram",
     )(matrix, sketch)
-
-
-NB = 64
 
 
 def spread(v):
@@ -290,28 +289,29 @@
     return jnp.concatenate(out, 0)
 
 
-def cholesky_inverse(gram, linv, work):
-    n, nb = gram.shape[0], NB
+def cholesky_inverse(gram, work, use):
+    n, nb = gram.shape[0], 64
     same = lax.broadcasted_iota(jnp.int32, (n, n), 0) == lax.broadcasted_iota(jnp.int32, (n, n), 1)
     diagonal = jnp.where(same, gram, 0.0)
     unit = lax.rsqrt(jnp.sum(diagonal, 0, keepdims=True))
     work[:, 0:n] = gram * unit * lax.rsqrt(jnp.sum(diagonal, 1, keepdims=True))
     work[:, n:] = jnp.where(same, 1.0, 0.0)
-    linv[...] = jnp.zeros((n, n), F32)
     for lo in range(0, n, nb):
         hi = lo + nb
         first, last = lo // 128 * 128, -(-hi // 128) * 128
         rows = eliminate(jnp.concatenate([work[lo:hi, first:n], work[lo:hi, n:n + last]], 1), lo - first)
-        linv[lo:hi, 0:last] = rows[:, n - first:] * unit[:, 0:last]
         if hi < n:
             begin = hi // 128 * 128
             halves = split(rows)
-            left = tuple(v[:, begin - first:n - first] for v in halves)
             if begin > first:
                 halves = tuple(v[:, begin - first:] for v in halves)
-            less = dot3(left, halves, TN)[hi - begin:, :]
-            work[hi:n, begin:n] = work[hi:n, begin:n] - less[:, 0:n - begin]
-            work[hi:n, n:n + last] = work[hi:n, n:n + last] - less[:, n - begin:]
+            for top in (hi,) if hi + nb == n else (hi, hi + nb):
+                end = hi + nb if top == hi else n
+                left = tuple(v[:, top - begin:end - begin] for v in halves)
+                less = dot3(left, halves, TN)
+                work[top:end, begin:n] = work[top:end, begin:n] - less[:, 0:n - begin]
+                work[top:end, n:n + last] = work[top:end, n:n + last] - less[:, n - begin:]
+        use(lo, rows[:, n - first:] * unit[:, 0:last])
 
 
 def upper(ref, i, j):
@@ -343,7 +343,7 @@
     return jnp.concatenate(out, 1)
 
 
-def finish_kernel(scale, g_high, g_low, st_high, st_low, a_hbm, basis_ref, coeffs_ref, work, linv, a_own, load_sem):
+def finish_kernel(scale, g_high, g_low, st_high, st_low, a_hbm, basis_ref, coeffs_ref, work, a_own, load_sem):
     load = pltpu.make_async_copy(a_hbm, a_own, load_sem)
     load.start()
     r = lax.axis_index("rows")
@@ -351,19 +351,25 @@
     power = split(times_gram((st_high[...], st_low[...]), high, low))
     ranged = times_gram(power, high, low)
     halves = split(ranged)
-    cholesky_inverse(dot3(halves, power, NT), linv, work)
-    inverse = split(linv[...])
-    factor = split(dot3(inverse, power, NN))
-    load.wait()
-    basis_ref[...] = dot3(split(a_own[...]), factor, NT) * scale
+    gram = dot3(halves, power, NT)
     width = coeffs_ref.shape[0]
     row = lax.broadcasted_iota(jnp.int32, (128, 768), 0)
     col = lax.broadcasted_iota(jnp.int32, (128, 768), 1)
     pick = jnp.where(col == row + r * width, 1.0, 0.0).astype(BF16)
     rest = (ranged - halves[0].astype(F32)) - halves[1].astype(F32)
-    mine = sum(lax.dot_general(pick, part, NT, preferred_element_type=F32)
-               for part in (halves[0], halves[1], rest.astype(BF16)))
-    coeffs_ref[...] = dot3(split(mine), inverse, NT)[0:width, :]
+    mine = split(sum(lax.dot_general(pick, part, NT, preferred_element_type=F32)
+                     for part in (halves[0], halves[1], rest.astype(BF16))))
+    load.wait()
+    range_rows = split(dot3(split(a_own[...]), power, NT) * scale)
+
+    def use(lo, rows):
+        nb, last = rows.shape
+        factor = split(rows)
+        for out, left in ((basis_ref, range_rows), (coeffs_ref, mine)):
+            value = dot3((left[0][:, 0:last], left[1][:, 0:last]), factor, NT)
+            out[:, lo:lo + nb] = value[0:out.shape[0], :]
+
+    cholesky_inverse(gram, work, use)
 
 
 def finish(operands, scale, width):
@@ -375,7 +381,6 @@
         out_specs=(vmem, vmem),
         scratch_shapes=[
             pltpu.VMEM((256, 512), F32),
-            pltpu.VMEM((256, 256), F32),
             pltpu.VMEM((256, 768), F32),
             pltpu.SemaphoreType.DMA,
         ],

time: 63.7 us -> 63 us (0.989)
  Pallas kernels: 62.9 us -> 62.2 us
    pallas_call x1, Pallas kernels: 13.2 us -> 12.3 us  [finish(): pl.pallas_call(functools.partial(finish_kernel, scale), out_shape=(jax.Sh...]
where the time goes in v4:
time: 63 us; the launch traced here: 62.9 us
  Pallas kernels  62.2 us (99%)
  between operations  0.65 us (1%)
    pallas_call x1, Pallas kernels, reduced_gram(): pl.pallas_call(reduce_kernel, out_shape=[jax.ShapeDtypeStruct((2 * NX, LI...  50 us
    pallas_call x1, Pallas kernels, finish(): pl.pallas_call(functools.partial(finish_kernel, scale), out_shape=(jax.Sh...  12.3 us

profile of v4, /device:TPU:1, one launch (start us, length us, event | category | flops | bytes accessed | tf_op | source)
XLA Modules:
  0.0 62.9 jit_solution(16973831653964090870)
XLA Ops:
  0.6 0.0 copy-start
  0.6 50.0 %reduce_gram.1 = (bf16[8,336,128]{2,1,0:T(8,128)(2,1)S(1)}, bf16[8,336,128]{2,1,0:T(8,128)(2,1)S(1)}, bf16[256,768]{1,0:T(8,128)(2,1)S(1)}, bf16[256,768]{1,0:T(8,128)(2,1)S(1)}) custom-call(f32[256,768]{1,0:T(8,128)} %a_hbm.3, f32[768,256]{1,0:T(8,128)} %s_hbm.1), custom_call_target="tpu_custom_call" | custom-call | tf_op jit(solution)/shard_map/reduce_gram/pallas_call | solution.py:217
  50.6 0.0 copy-done
  50.6 12.3 %finish.1 = (f32[256,256]{1,0:T(8,128)}, f32[12,256]{1,0:T(8,128)}) custom-call(bf16[2688,128]{1,0:T(8,128)(2,1)S(1)} %bitcast.3, bf16[2688,128]{1,0:T(8,128)(2,1)S(1)} %bitcast.4, bf16[256,768]{1,0:T(8,128)(2,1)S(1)} %get-tuple-element.10.st_high, bf16[256,768]{1,0:T(8,128)(2,1)S(1)} %get-tuple-element.11.st_low, f32[256,768]{1,0:T(8,128)S(1)} %copy-done), custom_call_target="tpu_custom_call" | custom-call | tf_op jit(solution)/shard_map/finish/pallas_call | solution.py:377
Async XLA Ops:
  0.6 50.0 %copy-start = (f32[256,768]{1,0:T(8,128)S(1)}, f32[256,768]{1,0:T(8,128)}, u32[]{:S(2)}) copy-start(f32[256,768]{1,0:T(8,128)} %a_hbm.3) | copy-start | bytes 2359300

commit v5 on v4

--- a/solution.py
+++ b/solution.py
@@ -47,7 +47,7 @@
 SUBS = tuple((pl.ds(p.start, p.size // 2), pl.ds(p.start + p.size // 2, p.size // 2)) for p in PARTS)
 
 
-def reduce_kernel(a_hbm, s_hbm, high, low, st_high, st_low, a_own, s_own, part, sib_in, relay_in, x_in, acc, z_in, y_in, zy, yz, gath, load_sem,
+def reduce_kernel(a_hbm, s_hbm, high, low, st_high, st_low, a_own, s_own, part, sib_in, relay_in, x_in, acc, z_in, y_in, zy, yz, gath, hand, load_sem,
                   sib_s, sib_r, rl_s, rl_r, x_s, x_r, z_s, z_r, y_s, y_r, zy_s, zy_r, yz_s, yz_r,
                   zg_s, zg_r, yg_s, yg_r, xg_s, xg_r, fw_s, fw_r):
     r = lax.axis_index("rows")
@@ -68,10 +68,23 @@
     load = pltpu.make_async_copy(a_hbm, a_own, load_sem.at[0])
     load.start()
     barrier = pltpu.get_barrier_semaphore()
-    for axis, n in (("x", NX), ("y", NY), ("z", NZ)):
-        for k in range(1, n):
-            pl.semaphore_signal(barrier, inc=1, device_id=other(axis, k)[1], device_id_type=MESH)
-    pl.semaphore_signal(barrier, inc=1, device_id=sibling, device_id_type=MESH)
+
+    @pl.when(c == 1)
+    def _():
+        pl.semaphore_signal(barrier, inc=1, device_id=sibling, device_id_type=MESH)
+
+    @pl.when(c == 0)
+    def _():
+        pl.semaphore_wait(barrier, 1)
+        pl.semaphore_signal(hand, inc=1, device_id=sibling, device_id_type=MESH)
+
+    @pl.when(c == 1)
+    def _():
+        pl.semaphore_wait(hand, 1)
+        for axis, n in (("x", NX), ("y", NY), ("z", NZ)):
+            for k in range(1, n):
+                pl.semaphore_signal(barrier, inc=1, device_id=other(axis, k)[1], device_id_type=MESH)
+
     load_s = pltpu.make_async_copy(s_hbm, s_own, load_sem.at[1])
     load_s.start()
 
@@ -94,8 +107,6 @@
         for j in range(i, 6):
             store_block(part, BLOCKS.index((i, j)), strip[:, 128 * j - lo:128 * j - lo + 128])
 
-    pl.semaphore_wait(barrier, 1 + (NX - 1) + (NY - 1) + (NZ - 1))
-
     right, to_right = other("x", 1)
     left, to_left = other("x", 3)
     across, _ = other("x", 2)
@@ -115,6 +126,15 @@
     def one_step(h, way, n, to=sibling):
         rows = SUBS[h][n]
         return part.at[c, (right, left)[way], rows], x_in.at[way, rows], x_s.at[h, way, n], x_r.at[h, way, n], to
+
+    @pl.when(c == 1)
+    def _():
+        pl.semaphore_wait(barrier, (NX - 1) + (NY - 1) + (NZ - 1))
+        pl.semaphore_signal(hand, inc=1, device_id=sibling, device_id_type=MESH)
+
+    @pl.when(c == 0)
+    def _():
+        pl.semaphore_wait(hand, 1)
 
     for h in range(2):
         add_sibling(h, across)
@@ -232,6 +252,7 @@
             pltpu.VMEM((8, PIECE, 128), F32),
             pltpu.VMEM((8, PIECE, 128), F32),
             pltpu.VMEM((2, NX, HELD, 128), F32),
+            pltpu.SemaphoreType.REGULAR,
             dma(2),
             dma(2, 4), dma(2, 4), dma(2, 2), dma(2, 2), dma(2, 2, 2), dma(2, 2, 2), dma(7), dma(7), dma(7), dma(7),
             dma(7), dma(8), dma(7), dma(8), dma(7), dma(8), dma(7), dma(8),

time: 63 us -> 61 us (0.968)
  Pallas kernels: 62.2 us -> 60.2 us
    pallas_call x1, Pallas kernels: 50 us -> 48 us  [reduced_gram(): pl.pallas_call(reduce_kernel, out_shape=[jax.ShapeDtypeStruct((2 * NX, LI...]
where the time goes in v5:
time: 61 us; the launch traced here: 60.9 us
  Pallas kernels  60.2 us (99%)
  between operations  0.65 us (1%)
    pallas_call x1, Pallas kernels, reduced_gram(): pl.pallas_call(reduce_kernel, out_shape=[jax.ShapeDtypeStruct((2 * NX, LI...  48 us
    pallas_call x1, Pallas kernels, finish(): pl.pallas_call(functools.partial(finish_kernel, scale), out_shape=(jax.Sh...  12.3 us

profile of v5, /device:TPU:1, one launch (start us, length us, event | category | flops | bytes accessed | tf_op | source)
XLA Modules:
  0.0 60.9 jit_solution(10811725681328214530)
XLA Ops:
  0.6 0.0 copy-start
  0.6 48.0 %reduce_gram.1 = (bf16[8,336,128]{2,1,0:T(8,128)(2,1)S(1)}, bf16[8,336,128]{2,1,0:T(8,128)(2,1)S(1)}, bf16[256,768]{1,0:T(8,128)(2,1)S(1)}, bf16[256,768]{1,0:T(8,128)(2,1)S(1)}) custom-call(f32[256,768]{1,0:T(8,128)} %a_hbm.3, f32[768,256]{1,0:T(8,128)} %s_hbm.1), custom_call_target="tpu_custom_call" | custom-call | tf_op jit(solution)/shard_map/reduce_gram/pallas_call | solution.py:237
  48.6 0.0 copy-done
  48.6 12.3 %finish.1 = (f32[256,256]{1,0:T(8,128)}, f32[12,256]{1,0:T(8,128)}) custom-call(bf16[2688,128]{1,0:T(8,128)(2,1)S(1)} %bitcast.3, bf16[2688,128]{1,0:T(8,128)(2,1)S(1)} %bitcast.4, bf16[256,768]{1,0:T(8,128)(2,1)S(1)} %get-tuple-element.10.st_high, bf16[256,768]{1,0:T(8,128)(2,1)S(1)} %get-tuple-element.11.st_low, f32[256,768]{1,0:T(8,128)S(1)} %copy-done), custom_call_target="tpu_custom_call" | custom-call | tf_op jit(solution)/shard_map/finish/pallas_call | solution.py:398
Async XLA Ops:
  0.6 48.0 %copy-start = (f32[256,768]{1,0:T(8,128)S(1)}, f32[256,768]{1,0:T(8,128)}, u32[]{:S(2)}) copy-start(f32[256,768]{1,0:T(8,128)} %a_hbm.3) | copy-start | bytes 2359300

commit v6 on v5

--- a/solution.py
+++ b/solution.py
@@ -364,7 +364,8 @@
     return jnp.concatenate(out, 1)
 
 
-def finish_kernel(scale, g_high, g_low, st_high, st_low, a_hbm, basis_ref, coeffs_ref, work, a_own, load_sem):
+def finish_kernel(scale, g_high, g_low, st_high, st_low, a_hbm, basis_hbm, coeffs_ref,
+                  work, basis_ref, a_own, load_sem, store_sem):
     load = pltpu.make_async_copy(a_hbm, a_own, load_sem)
     load.start()
     r = lax.axis_index("rows")
@@ -383,14 +384,22 @@
     load.wait()
     range_rows = split(dot3(split(a_own[...]), power, NT) * scale)
 
+    def store(n):
+        columns = pl.ds(128 * n, 128)
+        return pltpu.make_async_copy(basis_ref.at[:, columns], basis_hbm.at[:, columns], store_sem.at[n])
+
     def use(lo, rows):
         nb, last = rows.shape
         factor = split(rows)
         for out, left in ((basis_ref, range_rows), (coeffs_ref, mine)):
             value = dot3((left[0][:, 0:last], left[1][:, 0:last]), factor, NT)
             out[:, lo:lo + nb] = value[0:out.shape[0], :]
+        if (lo + nb) % 128 == 0:
+            store((lo + nb) // 128 - 1).start()
 
     cholesky_inverse(gram, work, use)
+    for n in range(2):
+        store(n).wait()
 
 
 def finish(operands, scale, width):
@@ -399,11 +408,13 @@
         functools.partial(finish_kernel, scale),
         out_shape=(jax.ShapeDtypeStruct((256, 256), F32), jax.ShapeDtypeStruct((width, 256), F32)),
         in_specs=[vmem] * 4 + [pl.BlockSpec(memory_space=pltpu.HBM)],
-        out_specs=(vmem, vmem),
+        out_specs=(pl.BlockSpec(memory_space=pltpu.HBM), vmem),
         scratch_shapes=[
             pltpu.VMEM((256, 512), F32),
+            pltpu.VMEM((256, 256), F32),
             pltpu.VMEM((256, 768), F32),
             pltpu.SemaphoreType.DMA,
+            pltpu.SemaphoreType.DMA((2,)),
         ],
         compiler_params=pltpu.CompilerParams(vmem_limit_bytes=40 * 1024 * 1024),
         name="finish",

time: 61 us -> 61.6 us (level)
  no operation moved by 1% of the time
where the time goes in v6:
time: 61.6 us; the launch traced here: 61.5 us
  Pallas kernels  60.8 us (99%)
  between operations  0.65 us (1%)
    pallas_call x1, Pallas kernels, reduced_gram(): pl.pallas_call(reduce_kernel, out_shape=[jax.ShapeDtypeStruct((2 * NX, LI...  48 us
    pallas_call x1, Pallas kernels, finish(): pl.pallas_call(functools.partial(finish_kernel, scale), out_shape=(jax.Sh...  12.8 us

profile of v6, /device:TPU:1, one launch (start us, length us, event | category | flops | bytes accessed | tf_op | source)
XLA Modules:
  0.0 61.5 jit_solution(764858616621452421)
XLA Ops:
  0.6 0.0 copy-start
  0.6 48.0 %reduce_gram.1 = (bf16[8,336,128]{2,1,0:T(8,128)(2,1)S(1)}, bf16[8,336,128]{2,1,0:T(8,128)(2,1)S(1)}, bf16[256,768]{1,0:T(8,128)(2,1)S(1)}, bf16[256,768]{1,0:T(8,128)(2,1)S(1)}) custom-call(f32[256,768]{1,0:T(8,128)} %a_hbm.3, f32[768,256]{1,0:T(8,128)} %s_hbm.1), custom_call_target="tpu_custom_call" | custom-call | tf_op jit(solution)/shard_map/reduce_gram/pallas_call | solution.py:237
  48.6 0.0 copy-done
  48.6 12.8 %finish.1 = (f32[256,256]{1,0:T(8,128)}, f32[12,256]{1,0:T(8,128)}) custom-call(bf16[2688,128]{1,0:T(8,128)(2,1)S(1)} %bitcast.3, bf16[2688,128]{1,0:T(8,128)(2,1)S(1)} %bitcast.4, bf16[256,768]{1,0:T(8,128)(2,1)S(1)} %get-tuple-element.10.st_high, bf16[256,768]{1,0:T(8,128)(2,1)S(1)} %get-tuple-element.11.st_low, f32[256,768]{1,0:T(8,128)S(1)} %copy-done), custom_call_target="tpu_custom_call" | custom-call | tf_op jit(solution)/shard_map/finish/pallas_call | solution.py:407
Async XLA Ops:
  0.6 48.0 %copy-start = (f32[256,768]{1,0:T(8,128)S(1)}, f32[256,768]{1,0:T(8,128)}, u32[]{:S(2)}) copy-start(f32[256,768]{1,0:T(8,128)} %a_hbm.3) | copy-start | bytes 2359300
